TPU v7x, 32 devices: a whole 2x2x4 slice. The times are simulated.
32 devices in a mesh: blk: 2 (over x), tile: 16 (over z, y, core).
Axes of the slice: x: 2, y: 2, z: 4, core: 2. Of those that a mesh axis runs over, the one named last changes fastest.
Arguments:
- forward: float32 [2, 1024, 16384], P(None, 'blk', 'tile'), may hold values from -6 to 6
- backward: float32 [2, 1024, 16384], P(None, 'blk', 'tile'), may hold values from -6 to 6
- phase: float32 [16, 1024], P('tile'), may hold values from -3.140625 to 3.140625
- footprint: int32 [16, 16], P('blk', 'tile'), may hold values 0 or 1
- groups: int32 [1024], replicated, may hold values from 0 to 44
Outputs:
- margin: float32 [2, 1024, 1024], P(None, 'blk', 'tile')
- gradient: float32 [16, 1024], P('tile', 'blk')
All inputs are finite; a program needn't handle non-finite values. No bound on the sum of `footprint` on one device may be relied on, other than what follows from the above.
Results may differ from a plain program's by a relative error of at most 0.00016.
Values sent between devices are 32-bit elements; how exact they have to be, the bound alone decides.
A program may use at most 320 MiB of HBM per device.

v0:
```python
import math

import jax
import jax.numpy as jnp
from jax import lax
from jax.sharding import PartitionSpec as P

MODES = 1024
BLOCK = 64


highest = lax.Precision.HIGHEST
cross_weight = 0.05


def pair_margin(left_fields, right_fields):
    left_count = left_fields.shape[1]
    right_count = right_fields.shape[1]
    stacked = lax.dot_general(
        left_fields.reshape(2 * left_count, -1),
        right_fields.reshape(2 * right_count, -1),
        (((1,), (1,)), ((), ())),
        precision=highest,
        preferred_element_type=jnp.float32,
    )
    real_part = stacked[:left_count, :right_count] + stacked[left_count:, right_count:]
    imag_part = stacked[:left_count, right_count:] - stacked[left_count:, :right_count]
    return jnp.stack([real_part, imag_part])


def response(coupled, fields):
    source_count = coupled.shape[1]
    target_count = coupled.shape[2]
    mixing = jnp.stack(
        [
            jnp.concatenate([coupled[0], -coupled[1]], 0),
            jnp.concatenate([coupled[1], coupled[0]], 0),
        ],
        axis=2,
    ).reshape(2 * source_count, 2 * target_count)
    product = lax.dot_general(
        mixing,
        fields.reshape(2 * source_count, -1),
        (((0,), (0,)), ((), ())),
        precision=highest,
        preferred_element_type=jnp.float32,
    )
    return product.reshape(target_count, 2, -1)


def margin_rows(masked, portion):
    return pair_margin(masked, portion)


def response_rows(coupled_rows, masked):
    return response(coupled_rows, masked)


def body(forward, backward, phase, footprint, groups):
    local_modes = backward.shape[1]
    pixel_count = backward.shape[2]
    rows_here, width_here = phase.shape
    phase_cos = jnp.cos(phase).reshape(pixel_count)
    phase_sin = jnp.sin(phase).reshape(pixel_count)
    shifted = jnp.stack(
        [
            forward[0] * phase_cos - forward[1] * phase_sin,
            forward[0] * phase_sin + forward[1] * phase_cos,
        ]
    )
    tile_count = lax.axis_size("tile")
    inverse_root = 1.0 / math.sqrt(pixel_count * tile_count)
    grad_scale = 0.25 / math.sqrt(MODES)
    column_share = MODES // tile_count
    tile_offset = lax.axis_index("tile") * column_share
    mode_offset = lax.axis_index("blk") * local_modes
    row_gate = jnp.repeat(footprint[:, 0].astype(jnp.float32), BLOCK)
    masked = backward * row_gate[None, :, None]
    block_values = margin_rows(masked, lax.all_gather(shifted, "blk", axis=1, tiled=True))
    margin_full = lax.psum(block_values, "tile") * inverse_root
    margin_out = lax.dynamic_slice_in_dim(margin_full, tile_offset, column_share, 2)
    own_groups = lax.dynamic_slice_in_dim(groups, mode_offset, local_modes)
    weights = jnp.where(own_groups[:, None] == groups[None, :], 1.0, -cross_weight).astype(
        jnp.float32
    )
    coupled = margin_full * weights[None]
    portion = lax.all_gather(shifted, "blk", axis=1, tiled=True)
    reply = response_rows(coupled, masked)
    local_sum = jnp.sum(portion[1] * reply[:, 0] - portion[0] * reply[:, 1], axis=0)
    gradient = (
        lax.psum_scatter(
            local_sum.reshape(rows_here, width_here), "blk", scatter_dimension=1, tiled=True
        )
        * grad_scale
    )
    return (margin_out, gradient)


def solution(mesh):
    placed = (
        P(None, "blk", "tile"),
        P(None, "blk", "tile"),
        P("tile", None),
        P("blk", "tile"),
        P(),
    )
    return jax.shard_map(
        body,
        mesh=mesh,
        in_specs=placed,
        out_specs=(P(None, "blk", "tile"), P("tile", "blk")),
        check_vma=False,
    )
```

profile of v0, /device:TPU:0, one launch (start us, length us, event | category | flops | bytes accessed | tf_op | source)
XLA Modules:
  0.0 373.0 jit_solution(11038931709322511658)
XLA Ops:
  7.2 0.0 all-gather.2.cloned.1.call-start
  7.2 0.8 fusion.9
  8.0 2.8 multiply_subtract_fusion
  10.8 2.3 pad_maximum_fusion.1
  13.1 0.0 copy-start.1
  13.1 0.0 all-gather.2.cloned.1.call-update
  13.1 0.0 all-reduce.2.cloned.1.call-start
  13.2 0.6 copy-done.1
  13.8 0.1 broadcast_in_dim.14
  13.9 0.1 mul.82
  13.9 4.4 %broadcast_multiply_fusion.1 = f32[2,512,1024]{2,1,0:T(8,128)} fusion(f32[2,512,1024]{2,1,0:T(8,128)} %param.6, f32[512]{0:T(512)S(1)} %mul.82), kind=kLoop, calls=%fused_computation.25 | loop fusion | flops 1048576 | bytes 8390656 | tf_op jit(solution)/shard_map/mul | solution.py:78
  18.4 101.6 %all-gather.2.cloned.1.call-done = f32[2,1024,1024]{2,1,0:T(8,128)} async-done(((f32[2,512,1024]{2,1,0:T(8,128)}), f32[2,1024,1024]{2,1,0:T(8,128)}) %all-gather.2.cloned.1.call-update) | async-done | bytes 8388624 | tf_op jit(solution)/shard_map/all_gather | solution.py:79
  120.0 29.7 %fusion.10 = f32[1024,2048]{1,0:T(8,128)S(1)} fusion(f32[1024,1024]{1,0:T(8,128)} %bitcast.55, f32[2048,1024]{1,0:T(8,128)} %bitcast.54), kind=kOutput, calls=%fused_computation.31 | convolution fusion | flops 25769803776 | bytes 20971520 | tf_op jit(solution)/shard_map/dot_general | solution.py:19
  149.8 1.4 fusion.7
  151.1 2.3 pad_maximum_fusion.2
  153.4 0.0 copy-start
  153.4 0.0 all-reduce.2.cloned.1.call-update
  153.4 0.2 reduce-scatter.4.cloned.1.call-start
  153.7 0.4 copy-done
  154.1 0.1 dynamic_slice.7
  154.2 0.3 select_multiply_fusion
  154.4 110.7 %all-reduce.2.cloned.1.call-done = f32[2,512,1024]{2,1,0:T(8,128)} async-done(((f32[2,512,1024]{2,1,0:T(8,128)}), f32[2,512,1024]{2,1,0:T(8,128)}) %all-reduce.2.cloned.1.call-update) | async-done | bytes 4194320 | tf_op jit(solution)/shard_map/psum | solution.py:80
  265.1 2.9 broadcast_multiply_fusion
  268.0 0.2 fusion.8
  268.2 1.7 slice_bitcast_fusion.4
  269.8 3.5 maximum_bitcast_fusion
  273.3 4.1 %pad_maximum_fusion = f32[1024,1024,2]{1,0,2:T(8,128)} fusion(f32[1024,1024,1]{1,0,2:T(8,128)S(1)} %get-tuple-element.15, f32[1024,1024,1]{1,0,2:T(8,128)S(1)} %get-tuple-element.14), kind=kLoop, calls=%fused_computation | loop fusion | flops 2097152 | bytes 16777216 | tf_op jit(solution)/shard_map/stack | solution.py:34
  277.4 13.4 %copy.11 = f32[1024,1024,2]{0,2,1:T(2,128)} copy(f32[1024,1024,2]{1,0,2:T(8,128)} %pad_maximum_fusion) | data formatting | bytes 16777216 | tf_op jit(solution)/shard_map/stack | solution.py:34
  290.8 10.9 %reshape.75 = f32[1024,2048]{0,1:T(8,128)} reshape(f32[1024,1024,2]{0,2,1:T(2,128)} %copy.11) | data formatting | bytes 16777216 | tf_op jit(solution)/shard_map/reshape | solution.py:40
  301.7 10.6 %dot_general.12 = f32[1024,2,1024]{2,1,0:T(2,128)} reshape(f32[2048,1024]{1,0:T(8,128)} %bitcast.53) | data formatting | bytes 16777216 | tf_op jit(solution)/shard_map/dot_general | solution.py:41
  312.2 33.2 %fusion = f32[1024,2,1024]{2,0,1:T(8,128)S(1)} fusion(f32[1024,1024,1]{1,0,2:T(8,128)} %bitcast.56, f32[1024,2,1024]{2,1,0:T(2,128)} %dot_general.12), kind=kOutput, calls=%fused_computation.1 | convolution fusion | flops 25769803776 | bytes 20971520 | tf_op jit(solution)/shard_map/dot_general | solution.py:41
  345.5 4.7 %fusion.4 = f32[1024]{0:T(1024)S(1)} fusion(f32[1024,2,1024]{2,0,1:T(8,128)S(1)} %fusion, f32[2,1024,1024]{2,1,0:T(8,128)} %all-gather.2.cloned.1.call-done), kind=kLoop, calls=%fused_computation.6 | loop fusion | flops 4193280 | bytes 16781312 | tf_op jit(solution)/shard_map/reduce_sum | solution.py:89
  350.2 1.0 copy.14
  351.2 0.0 reduce-scatter.4.cloned.1.call-update
  351.2 1.3 dynamic-slice_multiply_fusion
  352.5 0.9 copy.13
  353.3 11.5 %reduce-scatter.4.cloned.1.call-done = f32[512,1]{1,0:T(8,128)} async-done(((f32[1024,1]{1,0:T(8,128)}), f32[512,1]{1,0:T(8,128)}) %reduce-scatter.4.cloned.1.call-update) | async-done | bytes 2064
  364.8 1.1 copy.15
  365.9 0.6 broadcast_multiply_fusion.2
  (1 shorter events, 0.0 us)
Async XLA Ops:
  7.2 112.8 %all-gather.2.cloned.1.call-start = ((), (), s32[]{:S(2)}) async-start(), calls=%async_computation.1 | async-start | bytes 12582912 | tf_op jit(solution)/shard_map/all_gather | solution.py:79
  13.1 0.7 copy-start.1
  13.1 252.0 %all-reduce.2.cloned.1.call-start = ((), (), s32[]{:S(2)}) async-start(), calls=%async_computation.2 | async-start | bytes 8388608 | tf_op jit(solution)/shard_map/psum | solution.py:80
  153.4 0.7 copy-start
  153.4 211.4 %reduce-scatter.4.cloned.1.call-start = ((), (), s32[]{:S(2)}) async-start(), calls=%async_computation.3 | async-start | bytes 786432
Sparse Core Ops, SparseCore 0:
  13.3 106.6 all-gather.1
  153.5 111.5 all-reduce.1
  351.3 13.4 reduce-scatter.3
where the time goes:
time: 374 us; the launch traced here: 373 us
  waiting for transfers between devices  224 us (60%)
  matrix products  63 us (17%)
  local copies, waits for them, and re-layouts  41.5 us (11%)
  other arithmetic  30.6 us (8%)
  between operations  13.8 us (4%)
    psum x1, waiting for transfers between devices, body(): margin_full = lax.psum(block_values, 'tile') * inverse_root  111 us
    all_gather x1, waiting for transfers between devices, body(): lax.all_gather(shifted, 'blk', axis=1, tiled=True)  102 us
    dot_general x1, matrix products, response(): lax.dot_general(mixing, fields.reshape(2 * source_count, -1), (((0,), (0,...  33.2 us
    dot_general x1, matrix products, pair_margin(): lax.dot_general(left_fields.reshape(2 * left_count, -1), right_fields.res...  29.7 us
    another operation x1, local copies, waits for them, and re-layouts, response(): jnp.stack([jnp.concatenate([coupled[0], -coupled[1]], 0), jnp.concatenate...  13.4 us
    unnamed x4, waiting for transfers between devices  11.5 us
    reshape x1, local copies, waits for them, and re-layouts, response(): mixing = jnp.stack([jnp.concatenate([coupled[0], -coupled[1]], 0), jnp.co...  10.9 us
    dot_general x1, local copies, waits for them, and re-layouts, response(): lax.dot_general(mixing, fields.reshape(2 * source_count, -1), (((0,), (0,...  10.6 us
  transfers between devices with their start and end apart: 3, of which 3 were waited for; matrix products, arithmetic and copies ran while one was open for 2% of the time, Pallas kernels for 0%

commit v1 on v0

v1 whole, which is shorter than its diff:
```python
import math

import jax
import jax.numpy as jnp
from jax import lax
from jax.sharding import PartitionSpec as P

BLOCK = 64
CROSS = 0.05
CHUNKS = 2
HIGH = lax.Precision.HIGH


def pixels_dot(a, b):
    return lax.dot_general(
        a, b, (((1,), (1,)), ((), ())), precision=HIGH, preferred_element_type=jnp.float32
    )


def modes_dot(a, b):
    return lax.dot_general(
        a, b, (((0,), (0,)), ((), ())), precision=HIGH, preferred_element_type=jnp.float32
    )


def pair_margin(masked, fields):
    real = pixels_dot(masked[0], fields[0]) + pixels_dot(masked[1], fields[1])
    imag = pixels_dot(masked[0], fields[1]) - pixels_dot(masked[1], fields[0])
    return jnp.stack([real, imag])


def gradient_part(coupled, masked, fields):
    reply_re = modes_dot(coupled[0], masked[0]) - modes_dot(coupled[1], masked[1])
    reply_im = modes_dot(coupled[0], masked[1]) + modes_dot(coupled[1], masked[0])
    return jnp.sum(fields[1] * reply_re - fields[0] * reply_im, axis=0)


def body(forward, backward, phase, footprint, groups):
    local = backward.shape[1]
    pixels = backward.shape[2]
    modes = groups.shape[0]
    tiles = lax.axis_size("tile")
    share = modes // tiles
    b = lax.axis_index("blk")
    t = lax.axis_index("tile")
    c = jnp.cos(phase)
    s = jnp.sin(phase)
    swap = [(0, 1), (1, 0)]
    size = local // CHUNKS
    pieces, arriving = [], []
    for k in range(CHUNKS):
        f = forward[:, k * size : (k + 1) * size]
        piece = jnp.stack([f[0] * c - f[1] * s, f[0] * s + f[1] * c])
        pieces.append(piece)
        arriving.append(lax.ppermute(piece, "blk", swap))
    gate = jnp.repeat(footprint[:, 0].astype(jnp.float32), BLOCK)
    masked = backward * gate[None, :, None]
    inverse_root = 1.0 / math.sqrt(pixels * tiles)
    turned = jnp.roll(groups, -b * local)
    own_groups = turned[:local]
    margins = []
    own = jnp.concatenate(pieces, axis=1)
    for fields in [own] + arriving:
        part = pair_margin(masked, fields)
        if margins:
            corner = margins[-1][:1, :1, :1]
            part = jnp.where(jnp.isnan(corner), corner, part)
        margins.append(lax.psum(part, "tile"))
    total = jnp.zeros((pixels,), jnp.float32)
    scaled = []
    begin = 0
    for margin, fields in zip(margins, [own] + arriving):
        margin = margin * inverse_root
        scaled.append(margin)
        theirs = turned[begin : begin + fields.shape[1]]
        begin += fields.shape[1]
        weights = jnp.where(own_groups[:, None] == theirs[None, :], 1.0, -CROSS)
        total = total + gradient_part(margin * weights[None], masked, fields)
    whole = jnp.concatenate(scaled, axis=2)
    start = lax.rem(t * share + modes - b * local, modes)
    margin_out = lax.dynamic_slice_in_dim(whole, start, share, 2)
    half = pixels // 2
    halves = total.reshape(1, 2, half)
    mine = lax.dynamic_index_in_dim(halves, b, 1, keepdims=False)
    other = lax.dynamic_index_in_dim(halves, 1 - b, 1, keepdims=False)
    gradient = (mine + lax.ppermute(other, "blk", swap)) * (0.25 / math.sqrt(modes))
    return margin_out, gradient


def solution(mesh):
    placed = (
        P(None, "blk", "tile"),
        P(None, "blk", "tile"),
        P("tile", None),
        P("blk", "tile"),
        P(),
    )
    return jax.shard_map(
        body,
        mesh=mesh,
        in_specs=placed,
        out_specs=(P(None, "blk", "tile"), P("tile", "blk")),
        check_vma=False,
    )
```

time: 374 us -> 372 us (level)
  local copies, waits for them, and re-layouts: 41.5 us -> 4.97 us
  waiting for transfers between devices: 224 us -> 260 us
  other arithmetic: 30.6 us -> 24 us
  starting transfers between devices: 0.3 us -> 4.86 us
  matrix products: 63 us -> 58.7 us
    psum x1 -> x3, waiting for transfers between devices: 111 us -> 260 us  [body(): margins.append(lax.psum(part, 'tile'))]
    all_gather x1 -> x0, waiting for transfers between devices: 102 us -> none  [body(): lax.all_gather(shifted, 'blk', axis=1, tiled=True)]
    another operation x1 -> x0, local copies, waits for them, and re-layouts: 13.4 us -> none  [response(): jnp.stack([jnp.concatenate([coupled[0], -coupled[1]], 0), jnp.concatenate...]
    unnamed x4 -> x3, waiting for transfers between devices: 11.5 us -> 0.05 us
    reshape x1 -> x0, local copies, waits for them, and re-layouts: 10.9 us -> none  [response(): mixing = jnp.stack([jnp.concatenate([coupled[0], -coupled[1]], 0), jnp.co...]
    dot_general x1 -> x0, local copies, waits for them, and re-layouts: 10.6 us -> none  [response(): lax.dot_general(mixing, fields.reshape(2 * source_count, -1), (((0,), (0,...]
    another operation x5 -> x3, other arithmetic: 13.4 us -> 4.64 us  [the longest x2 3.11 us: body(): piece = jnp.stack([f[0] * c - f[1] * s, f[0] * s + f[1] * c])]
    reduce_sum x1 -> x0, other arithmetic: 4.69 us -> none  [body(): jnp.sum(portion[1] * reply[:, 0] - portion[0] * reply[:, 1], axis=0)]
  transfers between devices with their start and end apart: 3 -> 6, of which waited for: 3 -> 3; matrix products, arithmetic and copies ran while one was open for 2% -> 16% of each run, Pallas kernels for 0% -> 0%
where the time goes in v1:
time: 372 us; the launch traced here: 370 us
  waiting for transfers between devices  260 us (70%)
  matrix products  58.7 us (16%)
  other arithmetic  24 us (6%)
  between operations  16.9 us (5%)
  local copies, waits for them, and re-layouts  4.97 us (1%)
  starting transfers between devices  4.86 us (1%)
    psum x3, waiting for transfers between devices, body(): margins.append(lax.psum(part, 'tile'))  260 us
    dot_general x12, matrix products, pixels_dot(): lax.dot_general(a, b, (((1,), (1,)), ((), ())), precision=HIGH, preferred...  35.3 us
    dot_general x12, matrix products, modes_dot(): lax.dot_general(a, b, (((0,), (0,)), ((), ())), precision=HIGH, preferred...  23.4 us
    mul x5, other arithmetic, body(): total = total + gradient_part(margin * weights[None], masked, fields)  9.36 us
  transfers between devices with their start and end apart: 6, of which 3 were waited for; matrix products, arithmetic and copies ran while one was open for 16% of the time, Pallas kernels for 0%

profile of v1, /device:TPU:0, one launch (start us, length us, event | category | flops | bytes accessed | tf_op | source)
XLA Modules:
  0.0 369.8 jit_solution(1624073888819427090)
XLA Ops:
  7.2 0.0 all-reduce.4.cloned.1.call-start
  7.2 0.7 convert_bitcast_fusion
  7.9 0.1 broadcast_in_dim.64
  7.9 0.1 mul.153
  8.0 0.8 fusion.36
  8.8 0.0 copy-start.9
  8.8 3.0 multiply_subtract_fusion.1
  11.9 0.4 copy-done.9
  12.3 0.8 maximum_maximum_fusion
  13.1 1.9 fusion
  15.0 1.9 fusion.1
  16.9 1.9 fusion.7
  18.9 1.9 fusion.5
  20.8 1.5 pad_maximum_fusion.2
  22.4 0.0 all-reduce.4.cloned.1.call-update
  22.4 0.3 all-reduce.6.cloned.1.call-start
  22.7 1.6 pad_maximum_fusion.1
  24.3 2.9 collective-permute-start.1
  27.2 1.5 pad_maximum_fusion
  28.8 0.0 collective-permute-start
  28.8 0.1 fusion.33
  28.9 0.2 select_multiply_fusion
  29.0 1.2 select_multiply_fusion.2
  30.2 93.1 %all-reduce.4.cloned.1.call-done = f32[2,512,512]{2,1,0:T(8,128)} async-done(((f32[2,512,512]{2,1,0:T(8,128)}), f32[2,512,512]{2,1,0:T(8,128)}) %all-reduce.4.cloned.1.call-update) | async-done | bytes 2097168 | tf_op jit(solution)/shard_map/psum | solution.py:68
  123.3 1.2 slice.147
  125.8 3.7 %broadcast_multiply_fusion.1 = (f32[2,512,512]{2,1,0:T(8,128)S(1)}, f32[2,512,512]{2,1,0:T(8,128)}) fusion(f32[2,512,512]{2,1,0:T(8,128)} %all-reduce.4.cloned.1.call-done, f32[512,512]{1,0:T(8,128)S(1)} %select_multiply_fusion), kind=kLoop, calls=%fused_computation.49 | loop fusion | flops 1048576 | bytes 7340032 | tf_op jit(solution)/shard_map/mul | solution.py:78
  129.5 1.9 fusion.20
  131.4 1.9 fusion.22
  133.3 1.9 fusion.21
  135.2 0.3 copy-done.6
  135.5 2.3 subtract_reduce_fusion
  137.7 0.0 collective-permute-done
  137.8 2.2 fusion.24
  140.0 2.2 fusion.19
  142.3 13.4 %fusion.23 = f32[512,256]{1,0:T(8,128)S(1)} fusion(f32[2,256,1024]{2,1,0:T(8,128)} %collective-permute-done, f32[2,512,1024]{2,1,0:T(8,128)S(1)} %copy-done.1), kind=kOutput, calls=%fused_computation.59 | convolution fusion | flops 805306368 | bytes 3670016 | tf_op jit(solution)/shard_map/dot_general | solution.py:15
  155.6 2.2 fusion.18
  157.9 1.7 maximum_select_fusion
  159.6 0.0 all-reduce.6.cloned.1.call-update
  159.6 0.0 all-reduce.8.cloned.1.call-start
  159.6 0.0 collective-permute-done.1
  159.7 2.8 fusion.26
  162.4 2.6 fusion.25
  165.1 1.0 fusion.17
  166.1 1.0 fusion.16
  167.2 85.3 %all-reduce.6.cloned.1.call-done = f32[2,512,256]{2,1,0:T(8,128)} async-done(((f32[2,512,256]{2,1,0:T(8,128)}), f32[2,512,256]{2,1,0:T(8,128)}) %all-reduce.6.cloned.1.call-update) | async-done | bytes 1048592 | tf_op jit(solution)/shard_map/psum | solution.py:68
  252.4 1.2 slice.150
  254.9 1.7 maximum_select_fusion.1
  256.6 0.0 all-reduce.8.cloned.1.call-update
  256.7 1.6 broadcast_multiply_fusion.4
  258.3 2.8 fusion.30
  261.1 2.5 fusion.11
  263.6 1.2 fusion.28
  264.8 2.6 fusion.14
  267.4 82.0 %all-reduce.8.cloned.1.call-done = f32[2,512,256]{2,1,0:T(8,128)} async-done(((f32[2,512,256]{2,1,0:T(8,128)}), f32[2,512,256]{2,1,0:T(8,128)}) %all-reduce.8.cloned.1.call-update) | async-done | bytes 1048592 | tf_op jit(solution)/shard_map/psum | solution.py:68
  349.3 2.6 broadcast_multiply_fusion.3
  352.0 2.7 fusion.29
  354.7 1.2 fusion.27
  355.9 1.3 fusion.8
  357.1 1.4 fusion.15
  358.5 1.5 collective-permute-start.2
  360.1 1.5 fusion.32
  361.6 0.9 copy.7
  362.5 0.0 collective-permute-done.2
  362.5 0.6 fusion.34
  (24 shorter events, 0.1 us)
Async XLA Ops:
  7.2 116.1 %all-reduce.4.cloned.1.call-start = ((), (), s32[]{:S(2)}) async-start(), calls=%async_computation | async-start | bytes 4194304 | tf_op jit(solution)/shard_map/psum | solution.py:68
  8.8 3.5 copy-start.9
  11.9 1.2 copy-start.7
  13.1 5.8 %copy-start = (f32[2,512,1024]{2,1,0:T(8,128)}, f32[2,512,1024]{2,1,0:T(8,128)S(1)}, u32[]{:S(2)}) copy-start(f32[2,512,1024]{2,1,0:T(8,128)S(1)} %get-tuple-element.21) | copy-start | bytes 12582916
  13.1 5.8 %copy-start.5 = (f32[2,512,1024]{2,1,0:T(8,128)}, f32[2,512,1024]{2,1,0:T(8,128)S(1)}, u32[]{:S(2)}) copy-start(f32[2,512,1024]{2,1,0:T(8,128)S(1)} %get-tuple-element.20) | copy-start | bytes 12582916
  22.4 230.0 %all-reduce.6.cloned.1.call-start = ((), (), s32[]{:S(2)}) async-start(), calls=%async_computation.1 | async-start | bytes 2097152 | tf_op jit(solution)/shard_map/psum | solution.py:68
  22.7 4.5 %copy-start.8 = (f32[1,256,1024]{2,1,0:T(8,128)S(1)}, f32[1,256,1024]{2,1,0:T(8,128)}, u32[]{:S(2)}) copy-start(f32[1,256,1024]{2,1,0:T(8,128)} %copy-done.7) | copy-start | bytes 3145732
  24.3 4.5 %copy-start.10 = (s32[1024]{0:T(1024)S(1)}, s32[1024]{0:T(1024)}, u32[]{:S(2)}) copy-start(s32[1024]{0:T(1024)} %param.9) | copy-start | bytes 12292
  24.3 135.4 %collective-permute-start.1 = (f32[2,256,1024]{2,1,0:T(8,128)}, f32[2,256,1024]{2,1,0:T(8,128)S(1)}, u32[]{:S(2)}, u32[]{:S(2)}) collective-permute-start(f32[2,256,1024]{2,1,0:T(8,128)} %pad_maximum_fusion.1), channel_id=1, source_target_pairs={{0,16},{16,0},{1,17},{17,1},{2,18},{18,2},{3,19},{19,3},{4,20},{20... | collective-permute-start | bytes 6291464 | tf_op jit(solution)/shard_map/ppermute | solution.py:55
  28.8 109.0 %collective-permute-start = (f32[2,256,1024]{2,1,0:T(8,128)}, f32[2,256,1024]{2,1,0:T(8,128)}, u32[]{:S(2)}, u32[]{:S(2)}) collective-permute-start(f32[2,256,1024]{2,1,0:T(8,128)} %pad_maximum_fusion), channel_id=1, source_target_pairs={{0,16},{16,0},{1,17},{17,1},{2,18},{18,2},{3,19},{19,3},{4,20},{20... | collective-permute-start | bytes 6291464 | tf_op jit(solution)/shard_map/ppermute | solution.py:55
  125.8 3.7 %copy-start.1 = (f32[2,512,1024]{2,1,0:T(8,128)S(1)}, f32[2,512,1024]{2,1,0:T(8,128)}, u32[]{:S(2)}) copy-start(f32[2,512,1024]{2,1,0:T(8,128)} %copy-done) | copy-start | bytes 12582916
  133.3 2.2 copy-start.6
  159.6 189.7 %all-reduce.8.cloned.1.call-start = ((), (), s32[]{:S(2)}) async-start(), calls=%async_computation.2 | async-start | bytes 2097152 | tf_op jit(solution)/shard_map/psum | solution.py:68
  159.7 5.4 %copy-start.2 = (f32[2,512,1024]{2,1,0:T(8,128)S(1)}, f32[2,512,1024]{2,1,0:T(8,128)}, u32[]{:S(2)}) copy-start(f32[2,512,1024]{2,1,0:T(8,128)} %copy-done) | copy-start | bytes 12582916
  256.6 4.4 %copy-start.3 = (f32[2,512,1024]{2,1,0:T(8,128)S(1)}, f32[2,512,1024]{2,1,0:T(8,128)}, u32[]{:S(2)}) copy-start(f32[2,512,1024]{2,1,0:T(8,128)} %copy-done) | copy-start | bytes 12582916
  349.3 5.3 %copy-start.4 = (f32[2,512,1024]{2,1,0:T(8,128)S(1)}, f32[2,512,1024]{2,1,0:T(8,128)}, u32[]{:S(2)}) copy-start(f32[2,512,1024]{2,1,0:T(8,128)} %copy-done) | copy-start | bytes 12582916
  358.5 4.0 %collective-permute-start.2 = (f32[1,512]{1,0:T(1,128)S(1)}, f32[1,512]{1,0:T(1,128)S(1)}, u32[]{:S(2)}, u32[]{:S(2)}) collective-permute-start(f32[1,512]{1,0:T(1,128)S(1)} %dynamic-slice_bitcast_fusion), channel_id=1, source_target_pairs={{0,16},{16,0},{1,17},{17,1},{2,18},{18,2},{3,19},{19,3},{4,20},{20... | collective-permute-start | bytes 6152 | tf_op jit(solution)/shard_map/ppermute | solution.py:86
Sparse Core Ops, SparseCore 0:
  22.5 100.7 all-reduce.3
  159.7 92.6 all-reduce.5
  256.8 92.5 all-reduce.7
